TPU v7x, 32 devices: a whole 2x2x4 slice. The times are simulated.
32 devices in a mesh: img: 8 (over y, x, core), pose: 4 (over z).
Axes of the slice: x: 2, y: 2, z: 4, core: 2. Of those that a mesh axis runs over, the one named last changes fastest.
Arguments:
- images: bfloat16 [1024, 8192], P('img'), may hold values from -240 to 240
- shift_phase: float32 [8, 4096], replicated, may hold values from -3.140625 to 3.140625
- noise_weight: float32 [8192], replicated, may hold values from 0.005 to 0.05
- refs: bfloat16 [1536, 8192], P('pose', 'img'), may hold values from -6 to 6
- routing: int32 [49152, 1], P(('pose', 'img')), may hold values from 0 to 31; in each aligned block of 1536 rows (0 to 1535, 1536 to 3071, ...) at most 96 rows name the same one
- stencil: int32 [49152], P(('pose', 'img')), may hold values from 0 to 7
- interp: bfloat16 [32, 8, 256, 512], P(('img', 'pose')), may hold values from -48 to 48
Outputs:
- volume: float32 [32, 512], P(('img', 'pose'))
- evidence: float32 [1024], P('img')
Inputs may be any that keep to these rules, and one draw needn't show every extreme that they name: `routing`: among the rows of one device no brick is named more than 96 times, a bound that some block reaches there.
All inputs are finite; a program needn't handle non-finite values.
Results may differ from a plain program's by a relative error of at most 0.0052.
Values may be sent and summed in bfloat16 or wider, within the bound.
A program may use at most 192 MiB of HBM per device.

v0:
```python
import jax
import jax.numpy as jnp
from jax import lax
from jax.sharding import PartitionSpec as P

PIX = 4096
TRANS = 8
BLOCK = 128
STENCILS = 8


def translated(images, shift_phase, noise_weight):
    count = images.shape[0]
    blocks = images.astype(jnp.float32).reshape(count, 1, PIX // BLOCK, 2, BLOCK)
    real_part = blocks[:, :, :, 0, :]
    imag_part = blocks[:, :, :, 1, :]
    angles = shift_phase.reshape(1, TRANS, PIX // BLOCK, BLOCK)
    cosine = jnp.cos(angles)
    sine = jnp.sin(angles)
    new_real = real_part * cosine + imag_part * sine
    new_imag = imag_part * cosine - real_part * sine
    stacked = jnp.stack([new_real, new_imag], axis=3).reshape(count * TRANS, 2 * PIX)
    return (stacked * noise_weight[None, :]).astype(jnp.bfloat16)


def body(images, shift_phase, noise_weight, refs, routing, stencil, interp):
    weighted = translated(images, shift_phase, noise_weight)
    image_rows = weighted.shape[0]
    image_count = images.shape[0]
    pose_count = refs.shape[0]
    columns = lax.all_gather(refs, "img", axis=1, tiled=True)
    partial_scores = lax.dot_general(
        weighted, columns, (((1,), (1,)), ((), ())), preferred_element_type=jnp.float32
    )
    columns_wide = columns.astype(jnp.float32)
    half_norm = 0.5 * jnp.sum(columns_wide * columns_wide * noise_weight[None, :], axis=1)
    scores, half_norm = (partial_scores, half_norm)
    grouped = (scores - half_norm[None, :]).reshape(image_count, TRANS * pose_count)
    local_peak = jnp.max(grouped, axis=1)
    peak = lax.pmax(local_peak, "pose")
    expo = jnp.exp(grouped - peak[:, None])
    total = lax.psum(jnp.sum(expo, axis=1), "pose")
    evidence = peak + jnp.log(total)
    posterior = (expo / total[:, None]).astype(jnp.bfloat16).reshape(image_rows, pose_count)
    img_count = lax.axis_size("img")
    share = pose_count // img_count
    accum = lax.psum_scatter(
        lax.dot_general(
            posterior, weighted, (((0,), (0,)), ((), ())), preferred_element_type=jnp.float32
        ),
        "img",
        scatter_dimension=0,
        tiled=True,
    )
    block_rows = accum.astype(jnp.bfloat16).reshape(share * (PIX // BLOCK), 2 * BLOCK)
    pose_axis = lax.axis_size("pose")
    devices = img_count * pose_axis
    row_count = block_rows.shape[0]
    capacity = max(2, 2 * row_count // devices)
    target = routing[:, 0]
    one_hot = (target[:, None] == jnp.arange(devices, dtype=jnp.int32)[None, :]).astype(jnp.int32)
    before = jnp.cumsum(one_hot, axis=0) - one_hot
    slot_index = jnp.sum(before * one_hot, axis=1)
    rows_buffer = (
        jnp.zeros((devices, capacity, 2 * BLOCK), jnp.bfloat16)
        .at[target, slot_index]
        .set(block_rows)
    )
    stencil_buffer = (
        jnp.full((devices, capacity), STENCILS, jnp.int32).at[target, slot_index].set(stencil)
    )
    got_rows, got_stencil = (
        lax.all_to_all(rows_buffer, ("img", "pose"), split_axis=0, concat_axis=0, tiled=True),
        lax.all_to_all(stencil_buffer, ("img", "pose"), split_axis=0, concat_axis=0, tiled=True),
    )
    flat_rows = got_rows.reshape(devices * capacity, 2 * BLOCK)
    flat_stencil = got_stencil.reshape(devices * capacity)
    selector = (jnp.arange(STENCILS, dtype=jnp.int32)[:, None] == flat_stencil[None, :]).astype(
        jnp.bfloat16
    )
    gathered = jnp.dot(selector, flat_rows, preferred_element_type=jnp.float32).astype(jnp.bfloat16)
    gathered = gathered.reshape(1, STENCILS * 2 * BLOCK)
    matrices = interp.reshape(STENCILS * 2 * BLOCK, interp.shape[3])
    summed_volume = jnp.dot(gathered, matrices, preferred_element_type=jnp.float32)
    received = jnp.sum((flat_stencil < STENCILS).astype(jnp.float32))
    volume = summed_volume * lax.rsqrt(1.0 + received)
    return (volume, evidence)


def solution(mesh):
    return jax.shard_map(
        body,
        mesh=mesh,
        in_specs=(
            P("img", None),
            P(),
            P(),
            P("pose", "img"),
            P(("pose", "img"), None),
            P(("pose", "img")),
            P(("img", "pose"), None, None, None),
        ),
        out_specs=(P(("img", "pose"), None), P("img")),
        check_vma=False,
    )
```

profile of v0, /device:TPU:0, one launch (start us, length us, event | category | flops | bytes accessed | tf_op | source)
XLA Modules:
  0.0 356.5 jit_solution(8491974013925432447)
XLA Ops:
  7.2 0.7 all-gather.2.cloned.1.call-update
  7.9 0.0 reduce-scatter.2.cloned.1.call-start
  8.0 6.6 %reshape.134 = f32[128,1,32,2,128]{4,3,2,0,1:T(2,128)} reshape(bf16[128,8192]{1,0:T(8,128)(2,1)} %param.7) | data formatting | bytes 6291456 | tf_op jit(solution)/shard_map/reshape | solution.py:14
  14.6 0.5 cosine_bitcast_fusion
  15.1 7.9 %fusion.16 = (f32[128,1,32,1,128]{4,3,2,0,1:T(1,128)S(1)}, f32[128,1,32,1,128]{4,3,2,0,1:T(1,128)S(1)}) fusion(f32[128,1,32,2,128]{4,3,2,0,1:T(2,128)} %reshape.134), kind=kLoop, calls=%fused_computation.44 | loop fusion | bytes 8388608 | tf_op jit(solution)/shard_map/slice | solution.py:15
  23.0 38.2 %multiply_add_fusion = (f32[128,8,32,1,128]{4,3,2,1,0:T(1,128)}, f32[128,8,32,1,128]{4,3,2,1,0:T(1,128)}) fusion(f32[8,32,128]{2,1,0:T(8,128)S(1)} %copy.27, f32[128,32,128]{2,1,0:T(8,128)S(1)} %bitcast.43, f32[8,32,128]{2,1,0:T(8,128)S(1)} %copy.26, f32[128,32,128]{2,1,0:T(8,128)S(1)} %bitcast.42), kind=kLoop, calls=%fused_computation.5 | loop fusion | flops 25165824 | bytes 38010880 | tf_op jit(solution)/shard_map/add | solution.py:20
  61.2 35.4 %pad_maximum_fusion = f32[128,8,32,2,128]{4,3,2,1,0:T(2,128)} fusion(f32[128,8,32,1,128]{4,3,2,1,0:T(1,128)} %get-tuple-element.3, f32[128,8,32,1,128]{4,3,2,1,0:T(1,128)} %get-tuple-element.2), kind=kLoop, calls=%fused_computation.2 | loop fusion | flops 8388608 | bytes 67108864 | tf_op jit(solution)/shard_map/stack | solution.py:22
  96.7 41.8 %reshape.119 = f32[1024,8192]{1,0:T(8,128)} reshape(f32[128,8,32,2,128]{4,3,2,1,0:T(2,128)} %pad_maximum_fusion) | data formatting | bytes 67108864 | tf_op jit(solution)/shard_map/reshape | solution.py:22
  138.5 4.5 %multiply_reduce_fusion = f32[384]{0:T(512)S(1)} fusion(bf16[384,8192]{1,0:T(8,128)(2,1)} %all-gather.2.cloned.1.call-done, f32[8192]{0:T(1024)S(1)} %copy-done.1), kind=kLoop, calls=%fused_computation.6 | loop fusion | flops 12582528 | bytes 6325760 | tf_op jit(solution)/shard_map/reduce_sum | solution.py:36
  143.0 17.2 %subtract_reduce_fusion = (f32[1024]{0:T(1024)S(1)}, f32[1024,384]{0,1:T(8,128)}) fusion(f32[384]{0:T(512)S(1)} %broadcast_multiply_fusion.1, bf16[384,8192]{1,0:T(8,128)(2,1)} %all-gather.2.cloned.1.call-done, f32[1024,8192]{1,0:T(8,128)} %reshape.119, f32[8192]{0:T(1024)S(1)} %copy-done.1), kind=kOutput, calls=%fused_computation.11 | convolution fusion | flops 6460013568 | bytes 41457152 | tf_op jit(solution)/shard_map/dot_general | solution.py:32
  160.2 0.1 reduce_max.14
  160.2 0.1 reduce_max.18
  160.3 13.7 %pmax.7 = f32[128]{0:T(128)S(1)} all-reduce(f32[128]{0:T(128)S(1)} %reduce_max.18), channel_id=1, replica_groups=mesh['img'=8,'pose'=4] {'pose'}, use_global_device_ids=true, to_apply=%region_7.8 | all-reduce | flops 128 | bytes 1024 | tf_op jit(solution)/shard_map/pmax | solution.py:40
  174.0 0.1 sub.39
  174.1 0.1 sub.40
  174.2 1.7 fusion.2
  176.0 0.1 reduce_sum.49
  176.0 0.1 reduce_sum.50
  176.2 8.4 %psum.7 = f32[128]{0:T(128)S(1)} all-reduce(f32[128]{0:T(128)S(1)} %reduce_sum.50), channel_id=1, replica_groups=mesh['img'=8,'pose'=4] {'pose'}, use_global_device_ids=true, to_apply=%region_10.11 | all-reduce | flops 128 | bytes 1024 | tf_op jit(solution)/shard_map/psum | solution.py:42
  184.5 0.1 div.13
  184.6 0.1 div.14
  184.7 17.7 %fusion = f32[384,8192]{1,0:T(8,128)} fusion(f32[1024,8192]{1,0:T(8,128)} %reshape.119, f32[8192]{0:T(1024)S(1)} %copy-done.1, f32[1024,384]{0,1:T(8,128)} %get-tuple-element.11, f32[1024]{0:T(1024)S(1)} %div.14, f32[1024]{0:T(1024)S(1)} %sub.40, f32[384]{0:T(512)S(1)} %broadcast_multiply_fusion.1), kind=kOutput, calls=%fused_computation.7 | convolution fusion | flops 6460801024 | bytes 47752704 | tf_op jit(solution)/shard_map/dot_general | solution.py:48
  202.4 0.7 copy-done.3
  203.1 9.1 %reduce-window.6 = s32[32,12,128]{2,1,0:T(8,128)S(1)} reduce-window(s32[32,12,128]{2,1,0:T(8,128)S(1)} %fusion.9, s32[]{:T(128)} %constant.10.clone.1), window={size=1x1x128 pad=0_0x0_0x127_0}, to_apply=%region_0.0 | reduce-window | flops 6242304 | bytes 393220 | tf_op jit(solution)/shard_map/reduce-window
  212.2 0.1 slice.16
  212.4 0.2 copy.24
  212.6 0.1 copy.25
  212.7 0.1 broadcast_add_fusion
  212.8 0.1 fusion.12
  212.9 0.1 multiply_reduce_fusion.1
  213.0 0.1 and_reduce_fusion
  213.1 6.4 %scatter_custom_fusion = s32[3072]{0:T(1024)S(1)} fusion(s32[1536]{0:T(1024)S(1)} %broadcast_select_fusion, s32[1536]{0:T(1024)} %param.12, s32[]{:T(128)} %constant.9.clone.1), kind=kCustom, calls=%fused_computation.38 | custom fusion | bytes 12800
  219.5 0.7 all_to_all.9
  220.2 4.3 %all-to-all-start = ((s32[32,1,96]{2,1,0:T(1,128)}), s32[32,1,96]{2,1,0:T(1,128)S(1)}, u32[]{:S(2)}, u32[]{:S(2)}) async-start(s32[32,1,96]{2,1,0:T(1,128)} %all_to_all.9), calls=%async_computation | async-start | bytes 32768 | tf_op jit(solution)/shard_map/all_to_all | solution.py:74
  224.5 70.2 %reduce-scatter.2.cloned.1.call-done = f32[48,8192]{1,0:T(8,128)} async-done(((f32[384,8192]{1,0:T(8,128)}), f32[48,8192]{1,0:T(8,128)}) %reduce-scatter.2.cloned.1.call-update) | async-done | bytes 1572880 | tf_op jit(solution)/shard_map/reduce_scatter | solution.py:47
  294.7 1.5 convert_element_type.35
  296.2 1.2 reshape.143
  297.4 8.8 %scatter_custom_fusion.1 = bf16[3072,256]{1,0:T(8,128)(2,1)} fusion(s32[1536]{0:T(1024)S(1)} %broadcast_select_fusion, bf16[1536,256]{1,0:T(8,128)(2,1)} %reshape.143, bf16[]{:T(256)} %constant.4.clone.1), kind=kCustom, calls=%fused_computation.15 | custom fusion | bytes 1573376
  306.3 4.7 %all-to-all-start.1 = ((bf16[32,96,256]{2,1,0:T(8,128)(2,1)}), bf16[32,96,256]{2,1,0:T(8,128)(2,1)}, u32[]{:S(2)}, u32[]{:S(2)}) async-start(bf16[32,96,256]{2,1,0:T(8,128)(2,1)} %bitcast.44), calls=%async_computation.2 | async-start | bytes 3145728 | tf_op jit(solution)/shard_map/all_to_all | solution.py:73
  311.0 0.5 broadcast.152
  311.5 0.7 reduce.17
  312.2 0.1 eq.49
  312.3 0.6 convert_reduce_fusion
  313.6 0.5 log_add_fusion
  314.1 32.8 %all-to-all-done.1 = bf16[32,96,256]{2,1,0:T(8,128)(2,1)} async-done(((bf16[32,96,256]{2,1,0:T(8,128)(2,1)}), bf16[32,96,256]{2,1,0:T(8,128)(2,1)}, u32[]{:S(2)}, u32[]{:S(2)}) %all-to-all-start.1) | async-done | bytes 1572896 | tf_op jit(solution)/shard_map/all_to_all | solution.py:73
  346.9 1.7 fusion.3
  348.7 0.4 fusion.17
  349.0 0.6 broadcast_multiply_fusion
  (24 shorter events, 0.3 us)
Async XLA Ops:
  7.2 341.5 %copy-start = (bf16[1,8,256,512]{3,2,1,0:T(8,128)(2,1)S(1)}, bf16[1,8,256,512]{3,2,1,0:T(8,128)(2,1)}, u32[]{:S(2)}) copy-start(bf16[1,8,256,512]{3,2,1,0:T(8,128)(2,1)} %param.13) | copy-start | bytes 6291460
  7.2 7.4 %copy-start.2 = (f32[8,4096]{1,0:T(8,128)S(1)}, f32[8,4096]{1,0:T(8,128)}, u32[]{:S(2)}) copy-start(f32[8,4096]{1,0:T(8,128)} %param.8) | copy-start | bytes 393220
  7.2 131.3 %all-gather.2.cloned.1.call-start = ((), (), s32[]{:S(2)}) async-start(), calls=%async_computation.3 | async-start | bytes 7077888 | tf_op jit(solution)/shard_map/all_gather | solution.py:31
  7.9 286.8 %reduce-scatter.2.cloned.1.call-start = ((), (), s32[]{:S(2)}) async-start(), calls=%async_computation.4 | async-start | bytes 14155776 | tf_op jit(solution)/shard_map/reduce_scatter | solution.py:47
  96.6 41.8 %copy-start.1 = (f32[8192]{0:T(1024)S(1)}, f32[8192]{0:T(1024)}, u32[]{:S(2)}) copy-start(f32[8192]{0:T(1024)} %param.9) | copy-start | bytes 98308
  202.4 0.7 copy-start.3
  202.4 10.5 %copy-start.5 = (s32[2]{0:T(128)S(1)}, s32[2]{0:T(128)}, u32[]{:S(2)}) copy-start(s32[2]{0:T(128)} %constant.25) | copy-start | bytes 28
  202.4 10.6 %copy-start.4 = (s32[2]{0:T(128)S(1)}, s32[2]{0:T(128)}, u32[]{:S(2)}) copy-start(s32[2]{0:T(128)} %constant.28) | copy-start | bytes 28
  220.2 86.1 %all-to-all-start = ((s32[32,1,96]{2,1,0:T(1,128)}), s32[32,1,96]{2,1,0:T(1,128)S(1)}, u32[]{:S(2)}, u32[]{:S(2)}) async-start(s32[32,1,96]{2,1,0:T(1,128)} %all_to_all.9), calls=%async_computation | async-start | bytes 32768 | tf_op jit(solution)/shard_map/all_to_all | solution.py:74
  306.3 40.7 %all-to-all-start.1 = ((bf16[32,96,256]{2,1,0:T(8,128)(2,1)}), bf16[32,96,256]{2,1,0:T(8,128)(2,1)}, u32[]{:S(2)}, u32[]{:S(2)}) async-start(bf16[32,96,256]{2,1,0:T(8,128)(2,1)} %bitcast.44), calls=%async_computation.2 | async-start | bytes 3145728 | tf_op jit(solution)/shard_map/all_to_all | solution.py:73
Sparse Core Ops, SparseCore 0:
  9.9 48.2 all-gather.1
  202.6 92.0 reduce-scatter.1
where the time goes:
time: 359 us; the launch traced here: 356 us
  waiting for transfers between devices  104 us (29%)
  other arithmetic  93.6 us (26%)
  local copies, waits for them, and re-layouts  76.1 us (21%)
  matrix products  37 us (10%)
  blocking collectives  22.1 us (6%)
  between operations  15 us (4%)
  starting transfers between devices  9.08 us (3%)
    reduce_scatter x1, waiting for transfers between devices, body(): lax.psum_scatter(lax.dot_general(posterior, weighted, (((0,), (0,)), ((),...  70.2 us
    reshape x1, local copies, waits for them, and re-layouts, translated(): jnp.stack([new_real, new_imag], axis=3).reshape(count * TRANS, 2 * PIX)  41.8 us
    add x1, other arithmetic, translated(): new_real = real_part * cosine + imag_part * sine  38.2 us
    another operation x1, other arithmetic, translated(): jnp.stack([new_real, new_imag], axis=3).reshape(count * TRANS, 2 * PIX)  35.4 us
    all_to_all x1, waiting for transfers between devices, body(): lax.all_to_all(rows_buffer, ('img', 'pose'), split_axis=0, concat_axis=0,...  32.8 us
    dot_general x1, matrix products, body(): lax.dot_general(posterior, weighted, (((0,), (0,)), ((), ())), preferred_...  17.7 us
    dot_general x1, matrix products, body(): lax.dot_general(weighted, columns, (((1,), (1,)), ((), ())), preferred_el...  17.2 us
    unnamed x15, local copies, waits for them, and re-layouts  15.9 us
  transfers between devices with their start and end apart: 4, of which 2 were waited for; matrix products, arithmetic and copies ran while one was open for 45% of the time, Pallas kernels for 0%

commit v1 on v0

v1 whole, which is shorter than its diff:
```python
import functools

import jax
import jax.numpy as jnp
from jax import lax
from jax.experimental import pallas as pl
from jax.experimental.pallas import tpu as pltpu
from jax.sharding import PartitionSpec as P

MESH = pl.DeviceIdType.MESH
F32 = jnp.float32
BF16 = jnp.bfloat16
LANES = 128


def remote(src, dst, send_sem, recv_sem, device):
    return pltpu.make_async_remote_copy(
        src_ref=src,
        dst_ref=dst,
        send_sem=send_sem,
        recv_sem=recv_sem,
        device_id=device,
        device_id_type=MESH,
    )


def kernel(
    n,
    pn,
    trans,
    images,
    table,
    noise,
    refs,
    seg,
    interp,
    volume,
    evidence,
    cols,
    weighted,
    scores,
    post,
    seg_all,
    seg_t,
    norm_acc,
    stats,
    part,
    part16,
    rows_in,
    message,
    bricks_in,
    matrices,
    gather_send,
    gather_recv,
    seg_send,
    seg_recv,
    stat_send,
    stat_recv,
    rows_send,
    rows_recv,
    brick_send,
    brick_recv,
    local_sem,
):
    me = lax.axis_index("img")
    mine = lax.axis_index("pose")
    core = me % 2
    chip = me // 2
    chips = n // 2
    partner = chip * 2 + 1 - core
    count, width = images.shape
    poses, depth = refs.shape
    share = seg.shape[0]
    block2 = 2 * LANES
    nblk = width // block2
    stencils = interp.shape[0]

    fetch = pltpu.make_async_copy(interp, matrices, local_sem)
    fetch.start()

    barrier = pltpu.get_barrier_semaphore()
    for d in range(1, n):
        pl.semaphore_signal(
            barrier, inc=1, device_id={"img": (me + d) % n}, device_id_type=MESH
        )
    for d in range(1, pn):
        pl.semaphore_signal(
            barrier, inc=1, device_id={"pose": (mine + d) % pn}, device_id_type=MESH
        )
    pl.semaphore_wait(barrier, n - 1 + pn - 1)

    sends = []
    for d in range(1, chips):
        target = ((chip + d) % chips) * 2 + core
        copy = remote(
            refs, cols.at[me], gather_send.at[d - 1], gather_recv.at[me], {"img": target}
        )
        copy.start()
        sends.append(copy)
    copy = remote(
        refs, cols.at[me], gather_send.at[chips - 1], gather_recv.at[me], {"img": partner}
    )
    copy.start()
    sends.append(copy)
    for d in range(1, n):
        copy = remote(
            seg,
            seg_all.at[pl.ds(pl.multiple_of(me * share, 8), share)],
            seg_send.at[d - 1],
            seg_recv.at[me],
            {"img": (me + d) % n},
        )
        copy.start()
        sends.append(copy)
    seg_all[pl.ds(pl.multiple_of(me * share, 8), share), :] = seg[...]

    @pl.loop(0, nblk)
    def _(b):
        at = pl.multiple_of(b * block2, block2)
        half = pl.multiple_of(b * LANES, LANES)
        re = images[:, pl.ds(at, LANES)].astype(F32)
        im = images[:, pl.ds(at + LANES, LANES)].astype(F32)
        for t in range(trans):
            co_r = table[t : t + 1, pl.ds(half, LANES)]
            si_r = table[trans + t : trans + t + 1, pl.ds(half, LANES)]
            co_i = table[2 * trans + t : 2 * trans + t + 1, pl.ds(half, LANES)]
            si_i = table[3 * trans + t : 3 * trans + t + 1, pl.ds(half, LANES)]
            rows = pl.ds(t * count, count)
            weighted[rows, pl.ds(at, LANES)] = (re * co_r + im * si_r).astype(BF16)
            weighted[rows, pl.ds(at + LANES, LANES)] = (im * co_i - re * si_i).astype(BF16)

    norm_acc[...] = jnp.zeros_like(norm_acc)
    total_rows = trans * count
    tile = min(512, total_rows)

    def multiply(block, src, first):
        start = pl.multiple_of(src * depth, LANES)

        @pl.loop(0, total_rows // tile)
        def _(r):
            rows = pl.ds(pl.multiple_of(r * tile, tile), tile)
            product = lax.dot_general(
                weighted[rows, pl.ds(start, depth)],
                block[...],
                (((1,), (1,)), ((), ())),
                preferred_element_type=F32,
            )
            if first:
                scores[rows, :] = product
            else:
                scores[rows, :] += product

        for g in range(depth // LANES):
            values = block[:, g * LANES : (g + 1) * LANES].astype(F32)
            lane_noise = noise[:, pl.ds(pl.multiple_of(start + g * LANES, LANES), LANES)]
            norm_acc[...] += values * values * lane_noise

    for d in range(chips):
        other = (chip + chips - d) % chips
        near = other * 2 + core
        far = other * 2 + 1 - core
        if d == 0:
            multiply(refs, near, True)
        else:
            remote(
                refs, cols.at[near], gather_send.at[0], gather_recv.at[near], {"img": partner}
            ).wait_recv()
            copy = remote(
                cols.at[near],
                cols.at[near],
                gather_send.at[chips - 1 + d],
                gather_recv.at[near],
                {"img": partner},
            )
            copy.start()
            sends.append(copy)
            multiply(cols.at[near], near, False)
        remote(
            refs, cols.at[far], gather_send.at[0], gather_recv.at[far], {"img": partner}
        ).wait_recv()
        multiply(cols.at[far], far, False)

    norm = 0.5 * jnp.sum(norm_acc[...].T, axis=0, keepdims=True)
    peak_wide = None
    for t in range(trans):
        rows = pl.ds(t * count, count)
        value = scores[rows, :] - norm
        scores[rows, :] = value
        peak_wide = value if peak_wide is None else jnp.maximum(peak_wide, value)
    local_peak = jnp.max(peak_wide, axis=1, keepdims=True)
    sum_wide = jnp.zeros((count, poses), F32)
    for t in range(trans):
        rows = pl.ds(t * count, count)
        value = jnp.exp(scores[rows, :] - local_peak)
        scores[rows, :] = value
        sum_wide += value
    local_sum = jnp.sum(sum_wide, axis=1, keepdims=True)
    lane = lax.broadcasted_iota(jnp.int32, (count, LANES), 1)
    both = jnp.where(lane == 0, local_peak, jnp.where(lane == 1, local_sum, 0.0))
    stats[mine] = both.T[0:8, :]
    for d in range(1, pn):
        copy = remote(
            stats.at[mine],
            stats.at[mine],
            stat_send.at[d - 1],
            stat_recv.at[mine],
            {"pose": (mine + d) % pn},
        )
        copy.start()
        sends.append(copy)

    for d in range(1, n):
        src = (me + n - d) % n
        remote(
            seg,
            seg_all.at[pl.ds(pl.multiple_of(src * share, 8), share)],
            seg_send.at[0],
            seg_recv.at[src],
            {"img": partner},
        ).wait_recv()
    seg_t[...] = seg_all[...].T

    for d in range(1, pn):
        src = (mine + pn - d) % pn
        remote(
            stats.at[src], stats.at[src], stat_send.at[0], stat_recv.at[src],
            {"pose": (mine + 1) % pn},
        ).wait_recv()
    peak = stats[0][0:1, :]
    for p in range(1, pn):
        peak = jnp.maximum(peak, stats[p][0:1, :])
    total = jnp.zeros((1, count), F32)
    for p in range(pn):
        total += stats[p][1:2, :] * jnp.exp(stats[p][0:1, :] - peak)
    evidence[...] = peak + jnp.log(total)
    factor = jnp.exp(stats[mine][0:1, :] - peak) / total
    factor = jnp.broadcast_to(factor, (count, count)).T[:, 0:1]
    for t in range(trans):
        rows = pl.ds(t * count, count)
        value = scores[rows, :] * factor
        post[:, t * count : (t + 1) * count] = value.T.astype(BF16)

    segments = part.shape[0]
    part[...] = jnp.zeros_like(part)

    @pl.loop(0, nblk)
    def _(b):
        at = pl.multiple_of(b * block2, block2)
        sums = jnp.dot(post[...], weighted[:, pl.ds(at, block2)], preferred_element_type=F32)
        names = lax.broadcasted_iota(jnp.int32, (segments, poses), 0).astype(F32)
        chosen = jnp.where(names == seg_t[pl.ds(b, 1), :], 1.0, 0.0).astype(BF16)
        part[...] += jnp.dot(chosen, sums.astype(BF16), preferred_element_type=F32)

    part16[...] = part[...].astype(BF16)
    group = pn * stencils
    for d in range(1, n):
        target = (me + d) % n
        copy = remote(
            part16.at[pl.ds(pl.multiple_of(target * group, 16), group)],
            rows_in.at[me],
            rows_send.at[d - 1],
            rows_recv.at[me],
            {"img": target},
        )
        copy.start()
        sends.append(copy)
    summed = part[pl.ds(pl.multiple_of(me * group, 16), group), :]
    message[...] = jnp.zeros_like(message)
    for p in range(pn):
        low = ((me * pn + p) * stencils).astype(F32)
        named = seg_all[...]
        inside = jnp.where((named >= low) & (named < low + stencils), 1.0, 0.0)
        message[p, stencils : stencils + 1, 0:LANES] = jnp.sum(inside, axis=0, keepdims=True)
    for d in range(1, n):
        src = (me + n - d) % n
        remote(
            rows_in.at[src], rows_in.at[src], rows_send.at[0], rows_recv.at[src],
            {"img": partner},
        ).wait_recv()
        summed += rows_in[src].astype(F32)
    for p in range(pn):
        message[p, 0:stencils, :] = summed[p * stencils : (p + 1) * stencils, :]
    for d in range(1, pn):
        target = (mine + d) % pn
        copy = remote(
            message.at[target],
            bricks_in.at[mine],
            brick_send.at[d - 1],
            brick_recv.at[mine],
            {"pose": target},
        )
        copy.start()
        sends.append(copy)
    brick = message[mine]
    fetch.wait()
    for d in range(1, pn):
        src = (mine + pn - d) % pn
        remote(
            bricks_in.at[src], bricks_in.at[src], brick_send.at[0], brick_recv.at[src],
            {"pose": (mine + 1) % pn},
        ).wait_recv()
        brick += bricks_in[src]
    gathered = brick[0:stencils, :].astype(BF16).astype(F32)
    received = jnp.sum(brick[stencils : 2 * stencils, :])
    row = lax.broadcasted_iota(jnp.int32, gathered.shape, 0)
    out = jnp.zeros((stencils, volume.shape[1]), F32)
    for s in range(stencils):
        out += jnp.dot(
            jnp.where(row == s, gathered, 0.0).astype(BF16),
            matrices[s],
            preferred_element_type=F32,
        )
    scale = lax.rsqrt(jnp.full((1, volume.shape[1]), 1.0, F32) + received)
    volume[...] = jnp.sum(out, axis=0, keepdims=True) * scale
    for copy in sends:
        copy.wait_send()


def body(images, shift_phase, noise_weight, refs, routing, stencil, interp):
    n = lax.axis_size("img")
    pn = lax.axis_size("pose")
    count, width = images.shape
    trans, pixels = shift_phase.shape
    poses, depth = refs.shape
    stencils = interp.shape[1]
    segments = n * pn * stencils
    nblk = pixels // LANES
    share = poses // n
    cosine = jnp.cos(shift_phase)
    sine = jnp.sin(shift_phase)
    split = noise_weight.reshape(nblk, 2, LANES)
    real_noise = split[:, 0, :].reshape(1, pixels)
    imag_noise = split[:, 1, :].reshape(1, pixels)
    table = jnp.concatenate(
        [cosine * real_noise, sine * real_noise, cosine * imag_noise, sine * imag_noise], axis=0
    )
    seg = (routing[:, 0] * stencils + stencil).astype(F32).reshape(share, nblk)
    seg = jnp.pad(seg, ((0, 0), (0, LANES - nblk)), constant_values=-1.0)
    vmem = pl.BlockSpec(memory_space=pltpu.VMEM)
    dma = pltpu.SemaphoreType.DMA
    flops = 4 * trans * count * width * poses
    volume, evidence = pl.pallas_call(
        functools.partial(kernel, n, pn, trans),
        out_shape=(
            jax.ShapeDtypeStruct((1, interp.shape[3]), F32),
            jax.ShapeDtypeStruct((1, count), F32),
        ),
        in_specs=[vmem] * 5 + [pl.BlockSpec(memory_space=pl.ANY)],
        out_specs=(vmem, vmem),
        scratch_shapes=[
            pltpu.VMEM((n, poses, depth), BF16),
            pltpu.VMEM((trans * count, width), BF16),
            pltpu.VMEM((trans * count, poses), F32),
            pltpu.VMEM((poses, trans * count), BF16),
            pltpu.VMEM((poses, LANES), F32),
            pltpu.VMEM((LANES, poses), F32),
            pltpu.VMEM((poses, LANES), F32),
            pltpu.VMEM((pn, 8, count), F32),
            pltpu.VMEM((segments, 2 * LANES), F32),
            pltpu.VMEM((segments, 2 * LANES), BF16),
            pltpu.VMEM((n, pn * stencils, 2 * LANES), BF16),
            pltpu.VMEM((pn, 2 * stencils, 2 * LANES), F32),
            pltpu.VMEM((pn, 2 * stencils, 2 * LANES), F32),
            pltpu.VMEM(interp.shape[1:], BF16),
            dma((n,)),
            dma((n,)),
            dma((n,)),
            dma((n,)),
            dma((pn,)),
            dma((pn,)),
            dma((n,)),
            dma((n,)),
            dma((pn,)),
            dma((pn,)),
            dma,
        ],
        compiler_params=pltpu.CompilerParams(
            collective_id=0, has_side_effects=True, vmem_limit_bytes=56 * 1024 * 1024
        ),
        cost_estimate=pl.CostEstimate(
            flops=flops, bytes_accessed=8 * 1024 * 1024, transcendentals=trans * count * poses
        ),
    )(images, table, noise_weight.reshape(1, width), refs, seg, interp[0])
    return (volume, evidence.reshape(count))


def solution(mesh):
    return jax.shard_map(
        body,
        mesh=mesh,
        in_specs=(
            P("img", None),
            P(),
            P(),
            P("pose", "img"),
            P(("pose", "img"), None),
            P(("pose", "img")),
            P(("img", "pose"), None, None, None),
        ),
        out_specs=(P(("img", "pose"), None), P("img")),
        check_vma=False,
    )
```

time: 359 us -> 91.6 us (0.26)
  waiting for transfers between devices: 104 us -> 0 us
  other arithmetic: 93.6 us -> 0.89 us
  Pallas kernels: 0 us -> 84.5 us
  local copies, waits for them, and re-layouts: 76.1 us -> 5.28 us
  matrix products: 37 us -> 0 us
  blocking collectives: 22.1 us -> 0 us
  between operations: 15 us -> 0.69 us
  starting transfers between devices: 9.08 us -> 0 us
    pallas_call x0 -> x1, Pallas kernels: none -> 84.5 us  [body(): pl.pallas_call(functools.partial(kernel, n, pn, trans), out_shape=(jax.Sh...]
    reduce_scatter x1 -> x0, waiting for transfers between devices: 70.2 us -> none  [body(): lax.psum_scatter(lax.dot_general(posterior, weighted, (((0,), (0,)), ((),...]
    reshape x3 -> x1, local copies, waits for them, and re-layouts: 49.6 us -> 0.07 us  [body(): seg = (routing[:, 0] * stencils + stencil).astype(F32).reshape(share, nblk)]
    another operation x4 -> x0, other arithmetic: 44.7 us -> none  [the longest x1 35.4 us: translated(): jnp.stack([new_real, new_imag], axis=3).reshape(count * TRANS, 2 * PIX)]
    add x2 -> x0, other arithmetic: 38.7 us -> none  [the longest x1 38.2 us: translated(): new_real = real_part * cosine + imag_part * sine]
    dot_general x4 -> x0, matrix products: 37 us -> none  [the longest x1 17.7 us: body(): lax.dot_general(posterior, weighted, (((0,), (0,)), ((), ())), preferred_...]
    all_to_all x2 -> x0, waiting for transfers between devices: 32.8 us -> none  [the longest x1 32.8 us: body(): lax.all_to_all(rows_buffer, ('img', 'pose'), split_axis=0, concat_axis=0,...]
    pmax x1 -> x0, blocking collectives: 13.7 us -> none  [body(): peak = lax.pmax(local_peak, 'pose')]
  transfers between devices with their start and end apart: 4 -> 0, of which waited for: 2 -> 0; matrix products, arithmetic and copies ran while one was open for 45% -> 0% of each run, Pallas kernels for 0% -> 0%
where the time goes in v1:
time: 91.6 us; the launch traced here: 91.3 us
  Pallas kernels  84.5 us (92%)
  local copies, waits for them, and re-layouts  5.28 us (6%)
    pallas_call x1, Pallas kernels, body(): pl.pallas_call(functools.partial(kernel, n, pn, trans), out_shape=(jax.Sh...  84.5 us
    unnamed x6, local copies, waits for them, and re-layouts  2.36 us

profile of v1, /device:TPU:0, one launch (start us, length us, event | category | flops | bytes accessed | tf_op | source)
XLA Modules:
  0.0 91.3 jit_solution(16645455034207047346)
XLA Ops:
  0.6 0.0 copy-start.1
  0.6 0.0 copy-start
  0.7 1.4 %fusion = (f32[8,4096]{1,0:T(8,128)S(1)}, f32[8,4096]{1,0:T(8,128)S(1)}) fusion(f32[8,4096]{1,0:T(8,128)} %param.8), kind=kLoop, calls=%fused_computation.7 | loop fusion | bytes 393216 | tf_op jit(solution)/shard_map/cos | solution.py:329
  2.0 0.9 fusion.1
  2.9 0.8 pad_maximum_fusion.table
  3.8 0.0 copy-done.1
  3.8 0.0 copy-done
  3.8 0.1 reshape.22
  3.9 0.6 pad.4.seg
  4.5 84.5 %shard_map.86 = (f32[1,512]{1,0:T(1,128)}, f32[1,128]{1,0:T(1,128)}) custom-call(bf16[128,8192]{1,0:T(8,128)(2,1)} %images.1, f32[32,4096]{1,0:T(8,128)} %pad_maximum_fusion.table, f32[1,8192]{1,0:T(1,128)} %bitcast.9, bf16[384,1024]{1,0:T(8,128)(2,1)} %refs.1, f32[48,128]{1,0:T(8,128)} %pad.4.seg, bf16[8,256,512]{2,1,0:T(8,128)(2,1)} %bitcast.10), custom_call_target="tpu_custom_call" | custom-call | flops 12884901888 | bytes 8388608 | tf_op jit(solution)/shard_map/pallas_call | solution.py:342
  89.0 1.2 %copy.11 = f32[1,512]{1,0:T(1,128)} copy(f32[1,512]{1,0:T(1,128)} %get-tuple-element.18) | data formatting | bytes 4096
  90.2 1.1 %copy.12 = f32[128]{0:T(128)} copy(f32[128]{0:T(128)} %bitcast.11) | data formatting | bytes 1024
  (3 shorter events, 0.1 us)
Async XLA Ops:
  0.6 3.1 %copy-start.1 = (s32[1536,1]{0,1:T(1,128)S(1)}, s32[1536,1]{0,1:T(1,128)}, u32[]{:S(2)}) copy-start(s32[1536,1]{0,1:T(1,128)} %param.11) | copy-start | bytes 18436
  0.6 3.2 %copy-start = (s32[1536]{0:T(1024)S(1)}, s32[1536]{0:T(1024)}, u32[]{:S(2)}) copy-start(s32[1536]{0:T(1024)} %param.12) | copy-start | bytes 18436

commit v2 on v1

v2 whole, which is shorter than its diff:
```python
import functools

import jax
import jax.numpy as jnp
from jax import lax
from jax.experimental import pallas as pl
from jax.experimental.pallas import tpu as pltpu
from jax.sharding import PartitionSpec as P

MESH = pl.DeviceIdType.MESH
F32 = jnp.float32
BF16 = jnp.bfloat16
LANES = 128


def remote(src, dst, send_sem, recv_sem, device):
    return pltpu.make_async_remote_copy(
        src_ref=src,
        dst_ref=dst,
        send_sem=send_sem,
        recv_sem=recv_sem,
        device_id=device,
        device_id_type=MESH,
    )


def kernel(
    n,
    pn,
    images,
    phase,
    noise,
    refs,
    seg,
    interp,
    volume,
    evidence,
    cols,
    weighted,
    scores,
    post,
    seg_all,
    seg_t,
    norms,
    stats,
    part,
    part16,
    rows_in,
    message,
    bricks_in,
    matrices,
    own_send,
    pass_send,
    diag_send,
    gather_recv,
    seg_send,
    seg_recv,
    norm_send,
    norm_recv,
    stat_send,
    stat_recv,
    rows_send,
    rows_recv,
    brick_send,
    brick_recv,
    local_sem,
):
    me = lax.axis_index("img")
    mine = lax.axis_index("pose")
    core = me % 2
    chip = me // 2
    chips = n // 2
    partner = chip * 2 + 1 - core
    count, width = images.shape
    trans = phase.shape[0]
    poses, depth = refs.shape
    piece = depth // 2
    share = seg.shape[0]
    block2 = 2 * LANES
    nblk = width // block2
    stencils = interp.shape[0]
    sends = []

    def send(src, dst, send_sem, recv_sem, device):
        copy = remote(src, dst, send_sem, recv_sem, device)
        copy.start()
        sends.append(copy)

    fetch = pltpu.make_async_copy(interp, matrices, local_sem)
    fetch.start()

    barrier = pltpu.get_barrier_semaphore()
    for d in range(1, n):
        pl.semaphore_signal(
            barrier, inc=1, device_id={"img": (me + d) % n}, device_id_type=MESH
        )
    for d in range(1, pn):
        pl.semaphore_signal(
            barrier, inc=1, device_id={"pose": (mine + d) % pn}, device_id_type=MESH
        )
    pl.semaphore_wait(barrier, n - 1 + pn - 1)

    square = chips == 4
    if square:
        near_x = (chip + 1 - 2 * (chip % 2)) * 2 + core
        near_y = ((chip + 2) % 4) * 2 + core
        diag = (3 - chip) * 2 + core
        first_hops = [near_x, near_y]
    else:
        first_hops = [((chip + d) % chips) * 2 + core for d in range(1, chips)]

    def own_half(h):
        return refs.at[:, h * piece : (h + 1) * piece]

    for h in range(2):
        for k, target in enumerate(first_hops):
            send(
                own_half(h), cols.at[me, h], own_send.at[k, h], gather_recv.at[me, h],
                {"img": target},
            )
        send(
            own_half(h), cols.at[me, h], own_send.at[len(first_hops), h],
            gather_recv.at[me, h], {"img": partner},
        )
    for d in range(1, n):
        send(
            seg,
            seg_all.at[pl.ds(pl.multiple_of(me * share, 8), share)],
            seg_send.at[d - 1],
            seg_recv.at[me],
            {"img": (me + d) % n},
        )
    seg_all[pl.ds(pl.multiple_of(me * share, 8), share), :] = seg[...]

    lane_sum = jnp.zeros((poses, LANES), F32)
    for g in range(depth // LANES):
        values = refs[:, g * LANES : (g + 1) * LANES].astype(F32)
        lane_noise = noise[:, pl.ds(pl.multiple_of(me * depth + g * LANES, LANES), LANES)]
        lane_sum += values * values * lane_noise
    norm_row = 0.5 * jnp.sum(lane_sum.T, axis=0, keepdims=True)
    norms[me] = jnp.broadcast_to(norm_row, (8, poses))
    for d in range(1, n):
        send(
            norms.at[me], norms.at[me], norm_send.at[d - 1], norm_recv.at[me],
            {"img": (me + d) % n},
        )

    @pl.loop(0, nblk)
    def _(b):
        at = pl.multiple_of(b * block2, block2)
        half = pl.multiple_of(b * LANES, LANES)
        re = images[:, pl.ds(at, LANES)].astype(F32)
        im = images[:, pl.ds(at + LANES, LANES)].astype(F32)
        angle = phase[:, pl.ds(half, LANES)]
        cosine = jnp.cos(angle)
        sine = jnp.sin(angle)
        real_noise = noise[:, pl.ds(at, LANES)]
        imag_noise = noise[:, pl.ds(at + LANES, LANES)]
        co_r = cosine * real_noise
        si_r = sine * real_noise
        co_i = cosine * imag_noise
        si_i = sine * imag_noise
        for t in range(trans):
            rows = pl.ds(t * count, count)
            one = slice(t, t + 1)
            weighted[rows, pl.ds(at, LANES)] = (re * co_r[one] + im * si_r[one]).astype(BF16)
            weighted[rows, pl.ds(at + LANES, LANES)] = (
                im * co_i[one] - re * si_i[one]
            ).astype(BF16)

    def multiply(block, src, h, first=False):
        start = pl.multiple_of(src * depth + h * piece, LANES)
        product = lax.dot_general(
            block,
            weighted[:, pl.ds(start, piece)],
            (((1,), (1,)), ((), ())),
            preferred_element_type=F32,
        )
        if first:
            scores[...] = product
        else:
            scores[...] += product

    def arrived(src, h):
        remote(
            own_half(h), cols.at[src, h], own_send.at[0, 0], gather_recv.at[src, h],
            {"img": partner},
        ).wait_recv()

    def hand_over(src, h, k):
        send(
            cols.at[src, h], cols.at[src, h], pass_send.at[k, h], gather_recv.at[src, h],
            {"img": partner},
        )

    def other_core(src):
        return (src // 2) * 2 + 1 - src % 2

    multiply(refs[:, 0:piece], me, 0, True)
    multiply(refs[:, piece : 2 * piece], me, 1)
    if square:
        arrived(near_x, 0)
        send(
            cols.at[near_x, 0], cols.at[near_x, 0], diag_send.at[0],
            gather_recv.at[near_x, 0], {"img": near_y},
        )
        hand_over(near_x, 0, 0)
        arrived(near_y, 0)
        hand_over(near_y, 0, 1)
        for h in range(2):
            arrived(partner, h)
            multiply(cols[partner, h], partner, h)
        multiply(cols[near_x, 0], near_x, 0)
        multiply(cols[near_y, 0], near_y, 0)
        for src in (near_x, near_y):
            arrived(other_core(src), 0)
            multiply(cols[other_core(src), 0], other_core(src), 0)
        arrived(near_y, 1)
        send(
            cols.at[near_y, 1], cols.at[near_y, 1], diag_send.at[1],
            gather_recv.at[near_y, 1], {"img": near_x},
        )
        hand_over(near_y, 1, 1)
        arrived(near_x, 1)
        hand_over(near_x, 1, 0)
        for src in (near_y, near_x):
            multiply(cols[src, 1], src, 1)
        for src in (near_y, near_x):
            arrived(other_core(src), 1)
            multiply(cols[other_core(src), 1], other_core(src), 1)
        for h in range(2):
            arrived(diag, h)
            hand_over(diag, h, 2)
        for src in (diag, other_core(diag)):
            for h in range(2):
                if src is not diag:
                    arrived(src, h)
                multiply(cols[src, h], src, h)
    else:
        for h in range(2):
            arrived(partner, h)
            multiply(cols[partner, h], partner, h)
        for k, src in enumerate(first_hops):
            for h in range(2):
                arrived(src, h)
                hand_over(src, h, k)
                multiply(cols[src, h], src, h)
                arrived(other_core(src), h)
                multiply(cols[other_core(src), h], other_core(src), h)

    norm_row = norms[me][0:1, :]
    for d in range(1, n):
        src = (me + n - d) % n
        remote(
            norms.at[src], norms.at[src], norm_send.at[0], norm_recv.at[src],
            {"img": partner},
        ).wait_recv()
        norm_row += norms[src][0:1, :]
    norm = jnp.broadcast_to(norm_row, (LANES, poses)).T
    local_peak = None
    for t in range(trans):
        value = scores[:, t * count : (t + 1) * count] - norm
        scores[:, t * count : (t + 1) * count] = value
        top = jnp.max(value, axis=0, keepdims=True)
        local_peak = top if local_peak is None else jnp.maximum(local_peak, top)
    local_sum = jnp.zeros((1, count), F32)
    for t in range(trans):
        value = jnp.exp(scores[:, t * count : (t + 1) * count] - local_peak)
        scores[:, t * count : (t + 1) * count] = value
        local_sum += jnp.sum(value, axis=0, keepdims=True)
    row = lax.broadcasted_iota(jnp.int32, (8, count), 0)
    stats[mine] = jnp.where(row == 0, local_peak, local_sum)
    for d in range(1, pn):
        send(
            stats.at[mine], stats.at[mine], stat_send.at[d - 1], stat_recv.at[mine],
            {"pose": (mine + d) % pn},
        )

    for d in range(1, n):
        src = (me + n - d) % n
        remote(
            seg,
            seg_all.at[pl.ds(pl.multiple_of(src * share, 8), share)],
            seg_send.at[0],
            seg_recv.at[src],
            {"img": partner},
        ).wait_recv()
    seg_t[...] = seg_all[...].T
    message[...] = jnp.zeros_like(message)
    for p in range(pn):
        low = ((me * pn + p) * stencils).astype(F32)
        named = seg_all[...]
        inside = jnp.where((named >= low) & (named < low + stencils), 1.0, 0.0)
        message[p, stencils : stencils + 1, 0:LANES] = jnp.sum(inside, axis=0, keepdims=True)

    for d in range(1, pn):
        src = (mine + pn - d) % pn
        remote(
            stats.at[src], stats.at[src], stat_send.at[0], stat_recv.at[src],
            {"pose": (mine + 1) % pn},
        ).wait_recv()
    peak = stats[0][0:1, :]
    for p in range(1, pn):
        peak = jnp.maximum(peak, stats[p][0:1, :])
    total = jnp.zeros((1, count), F32)
    for p in range(pn):
        total += stats[p][1:2, :] * jnp.exp(stats[p][0:1, :] - peak)
    evidence[...] = peak + jnp.log(total)
    factor = jnp.exp(local_peak - peak) / total
    for t in range(trans):
        at = slice(t * count, (t + 1) * count)
        post[:, at] = (scores[:, at] * factor).astype(BF16)

    segments = part.shape[0]
    part[...] = jnp.zeros_like(part)
    batch = 4 if nblk % 4 == 0 and segments <= 256 else 1

    @pl.loop(0, nblk // batch)
    def _(q):
        names = lax.broadcasted_iota(jnp.int32, (segments, poses), 0).astype(F32)
        rows, picks = [], []
        for u in range(batch):
            b = q * batch + u
            at = pl.multiple_of(b * block2, block2)
            sums = jnp.dot(post[...], weighted[:, pl.ds(at, block2)], preferred_element_type=F32)
            rows.append(sums.astype(BF16))
            picks.append(jnp.where(names == seg_t[pl.ds(b, 1), :], 1.0, 0.0).astype(BF16))
        part[...] += jnp.dot(
            jnp.concatenate(picks, axis=1),
            jnp.concatenate(rows, axis=0),
            preferred_element_type=F32,
        )

    part16[...] = part[...].astype(BF16)
    group = pn * stencils
    for d in range(1, n):
        target = (me + d) % n
        send(
            part16.at[pl.ds(pl.multiple_of(target * group, 16), group)],
            rows_in.at[me],
            rows_send.at[d - 1],
            rows_recv.at[me],
            {"img": target},
        )
    summed = part[pl.ds(pl.multiple_of(me * group, 16), group), :]
    for d in range(1, n):
        src = (me + n - d) % n
        remote(
            rows_in.at[src], rows_in.at[src], rows_send.at[0], rows_recv.at[src],
            {"img": partner},
        ).wait_recv()
        summed += rows_in[src].astype(F32)
    for p in range(pn):
        message[p, 0:stencils, :] = summed[p * stencils : (p + 1) * stencils, :]
    for d in range(1, pn):
        target = (mine + d) % pn
        send(
            message.at[target],
            bricks_in.at[mine],
            brick_send.at[d - 1],
            brick_recv.at[mine],
            {"pose": target},
        )
    brick = message[mine]
    fetch.wait()
    for d in range(1, pn):
        src = (mine + pn - d) % pn
        remote(
            bricks_in.at[src], bricks_in.at[src], brick_send.at[0], brick_recv.at[src],
            {"pose": (mine + 1) % pn},
        ).wait_recv()
        brick += bricks_in[src]
    gathered = brick[0:stencils, :].astype(BF16).astype(F32)
    received = jnp.sum(brick[stencils : 2 * stencils, :])
    row = lax.broadcasted_iota(jnp.int32, gathered.shape, 0)
    out = jnp.zeros((stencils, volume.shape[1]), F32)
    for s in range(stencils):
        out += jnp.dot(
            jnp.where(row == s, gathered, 0.0).astype(BF16),
            matrices[s],
            preferred_element_type=F32,
        )
    scale = lax.rsqrt(jnp.full((1, volume.shape[1]), 1.0, F32) + received)
    volume[...] = jnp.sum(out, axis=0, keepdims=True) * scale
    for copy in sends:
        copy.wait_send()


def body(images, shift_phase, noise_weight, refs, routing, stencil, interp):
    n = lax.axis_size("img")
    pn = lax.axis_size("pose")
    count, width = images.shape
    trans, pixels = shift_phase.shape
    poses, depth = refs.shape
    stencils = interp.shape[1]
    segments = n * pn * stencils
    nblk = pixels // LANES
    share = poses // n
    seg = (routing[:, 0] * stencils + stencil).astype(F32).reshape(share, nblk)
    seg = jnp.pad(seg, ((0, 0), (0, LANES - nblk)), constant_values=-1.0)
    vmem = pl.BlockSpec(memory_space=pltpu.VMEM)
    dma = pltpu.SemaphoreType.DMA
    flops = 4 * trans * count * width * poses
    volume, evidence = pl.pallas_call(
        functools.partial(kernel, n, pn),
        out_shape=(
            jax.ShapeDtypeStruct((1, interp.shape[3]), F32),
            jax.ShapeDtypeStruct((1, count), F32),
        ),
        in_specs=[vmem] * 5 + [pl.BlockSpec(memory_space=pl.ANY)],
        out_specs=(vmem, vmem),
        scratch_shapes=[
            pltpu.VMEM((n, 2, poses, depth // 2), BF16),
            pltpu.VMEM((trans * count, width), BF16),
            pltpu.VMEM((poses, trans * count), F32),
            pltpu.VMEM((poses, trans * count), BF16),
            pltpu.VMEM((poses, LANES), F32),
            pltpu.VMEM((LANES, poses), F32),
            pltpu.VMEM((n, 8, poses), F32),
            pltpu.VMEM((pn, 8, count), F32),
            pltpu.VMEM((segments, 2 * LANES), F32),
            pltpu.VMEM((segments, 2 * LANES), BF16),
            pltpu.VMEM((n, pn * stencils, 2 * LANES), BF16),
            pltpu.VMEM((pn, 2 * stencils, 2 * LANES), F32),
            pltpu.VMEM((pn, 2 * stencils, 2 * LANES), F32),
            pltpu.VMEM(interp.shape[1:], BF16),
            dma((n // 2, 2)),
            dma((n // 2, 2)),
            dma((2,)),
            dma((n, 2)),
            dma((n,)),
            dma((n,)),
            dma((n,)),
            dma((n,)),
            dma((pn,)),
            dma((pn,)),
            dma((n,)),
            dma((n,)),
            dma((pn,)),
            dma((pn,)),
            dma,
        ],
        compiler_params=pltpu.CompilerParams(
            collective_id=0, has_side_effects=True, vmem_limit_bytes=56 * 1024 * 1024
        ),
        cost_estimate=pl.CostEstimate(
            flops=flops, bytes_accessed=8 * 1024 * 1024, transcendentals=trans * count * poses
        ),
    )(images, shift_phase, noise_weight.reshape(1, width), refs, seg, interp[0])
    return (volume, evidence.reshape(count))


def solution(mesh):
    return jax.shard_map(
        body,
        mesh=mesh,
        in_specs=(
            P("img", None),
            P(),
            P(),
            P("pose", "img"),
            P(("pose", "img"), None),
            P(("pose", "img")),
            P(("img", "pose"), None, None, None),
        ),
        out_specs=(P(("img", "pose"), None), P("img")),
        check_vma=False,
    )
```

time: 91.6 us -> 69.5 us (0.76)
  Pallas kernels: 84.5 us -> 64.1 us
  local copies, waits for them, and re-layouts: 5.28 us -> 3.09 us
    pallas_call x1, Pallas kernels: 84.5 us -> 64.1 us  [body(): pl.pallas_call(functools.partial(kernel, n, pn), out_shape=(jax.ShapeDtyp...]
    cos x1 -> x0, local copies, waits for them, and re-layouts: 1.38 us -> none  [body(): cosine = jnp.cos(shift_phase)]
    unnamed x6 -> x2, local copies, waits for them, and re-layouts: 2.36 us -> 2.41 us
where the time goes in v2:
time: 69.5 us; the launch traced here: 69.3 us
  Pallas kernels  64.1 us (92%)
  local copies, waits for them, and re-layouts  3.09 us (4%)
  other arithmetic  1.42 us (2%)
    pallas_call x1, Pallas kernels, body(): pl.pallas_call(functools.partial(kernel, n, pn), out_shape=(jax.ShapeDtyp...  64.1 us
    unnamed x2, local copies, waits for them, and re-layouts  2.41 us

profile of v2, /device:TPU:0, one launch (start us, length us, event | category | flops | bytes accessed | tf_op | source)
XLA Modules:
  0.0 69.3 jit_solution(7168479549659049587)
XLA Ops:
  0.6 0.7 %multiply_reduce_fusion = s32[1536]{0:T(1024)S(1)} fusion(s32[1536,1]{0,1:T(1,128)} %param.11), kind=kLoop, calls=%fused_computation.1 | loop fusion | flops 1536 | bytes 12288 | tf_op jit(solution)/shard_map/mul | solution.py:399
  1.3 0.7 %add_convert_fusion = f32[1536]{0:T(1024)S(1)} fusion(s32[1536]{0:T(1024)S(1)} %multiply_reduce_fusion, s32[1536]{0:T(1024)} %param.12), kind=kLoop, calls=%fused_computation | loop fusion | flops 3072 | bytes 18432 | tf_op jit(solution)/shard_map/convert_element_type | solution.py:399
  2.1 0.1 reshape.16
  2.1 0.6 pad.4.seg
  2.7 64.1 %shard_map.86 = (f32[1,512]{1,0:T(1,128)}, f32[1,128]{1,0:T(1,128)}) custom-call(bf16[128,8192]{1,0:T(8,128)(2,1)} %images.1, f32[8,4096]{1,0:T(8,128)} %phase.1, f32[1,8192]{1,0:T(1,128)} %bitcast.4, bf16[384,1024]{1,0:T(8,128)(2,1)} %refs.1, f32[48,128]{1,0:T(8,128)} %pad.4.seg, bf16[8,256,512]{2,1,0:T(8,128)(2,1)} %bitcast.3), custom_call_target="tpu_custom_call" | custom-call | flops 12884901888 | bytes 8388608 | tf_op jit(solution)/shard_map/pallas_call | solution.py:404
  66.9 1.2 %copy.11 = f32[1,512]{1,0:T(1,128)} copy(f32[1,512]{1,0:T(1,128)} %get-tuple-element.8) | data formatting | bytes 4096
  68.1 1.2 %copy.12 = f32[128]{0:T(128)} copy(f32[128]{0:T(128)} %bitcast.5) | data formatting | bytes 1024

commit v3 on v2

--- a/solution.py
+++ b/solution.py
@@ -27,11 +27,13 @@
 def kernel(
     n,
     pn,
+    stencils,
     images,
     phase,
     noise,
     refs,
-    seg,
+    routing,
+    stencil,
     interp,
     volume,
     evidence,
@@ -39,8 +41,10 @@
     weighted,
     scores,
     post,
+    seg,
     seg_all,
     seg_t,
+    picks,
     norms,
     stats,
     part,
@@ -78,7 +82,7 @@
     share = seg.shape[0]
     block2 = 2 * LANES
     nblk = width // block2
-    stencils = interp.shape[0]
+    segments = part.shape[0]
     sends = []
 
     def send(src, dst, send_sem, recv_sem, device):
@@ -122,6 +126,8 @@
             own_half(h), cols.at[me, h], own_send.at[len(first_hops), h],
             gather_recv.at[me, h], {"img": partner},
         )
+    seg[...] = jnp.full(seg.shape, -1.0, F32)
+    seg[:, 0:nblk] = (routing[...] * stencils + stencil[...]).astype(F32)
     for d in range(1, n):
         send(
             seg,
@@ -196,6 +202,45 @@
     def other_core(src):
         return (src // 2) * 2 + 1 - src % 2
 
+    kept = picks.shape[0]
+
+    def choose(b):
+        names = lax.broadcasted_iota(jnp.int32, (segments, poses), 0).astype(F32)
+        return jnp.where(names == seg_t[pl.ds(b, 1), :], 1.0, 0.0).astype(BF16)
+
+    def prepare():
+        norm_row = norms[me][0:1, :]
+        for d in range(1, n):
+            src = (me + n - d) % n
+            remote(
+                norms.at[src], norms.at[src], norm_send.at[0], norm_recv.at[src],
+                {"img": partner},
+            ).wait_recv()
+            norm_row += norms[src][0:1, :]
+        norm = jnp.broadcast_to(norm_row, (LANES, poses)).T
+        for g in range(trans * count // LANES):
+            scores[:, g * LANES : (g + 1) * LANES] -= norm
+        for d in range(1, n):
+            src = (me + n - d) % n
+            remote(
+                seg,
+                seg_all.at[pl.ds(pl.multiple_of(src * share, 8), share)],
+                seg_send.at[0],
+                seg_recv.at[src],
+                {"img": partner},
+            ).wait_recv()
+        named = seg_all[...]
+        seg_t[...] = named.T
+        for p in range(pn):
+            low = ((me * pn + p) * stencils).astype(F32)
+            inside = jnp.where((named >= low) & (named < low + stencils), 1.0, 0.0)
+            stats[mine, 8 + p : 9 + p, :] = jnp.sum(inside, axis=0, keepdims=True)
+        if kept == nblk:
+
+            @pl.loop(0, nblk)
+            def _(b):
+                picks[b] = choose(b)
+
     multiply(refs[:, 0:piece], me, 0, True)
     multiply(refs[:, piece : 2 * piece], me, 1)
     if square:
@@ -215,6 +260,7 @@
         for src in (near_x, near_y):
             arrived(other_core(src), 0)
             multiply(cols[other_core(src), 0], other_core(src), 0)
+        prepare()
         arrived(near_y, 1)
         send(
             cols.at[near_y, 1], cols.at[near_y, 1], diag_send.at[1],
@@ -240,6 +286,7 @@
         for h in range(2):
             arrived(partner, h)
             multiply(cols[partner, h], partner, h)
+        prepare()
         for k, src in enumerate(first_hops):
             for h in range(2):
                 arrived(src, h)
@@ -248,19 +295,9 @@
                 arrived(other_core(src), h)
                 multiply(cols[other_core(src), h], other_core(src), h)
 
-    norm_row = norms[me][0:1, :]
-    for d in range(1, n):
-        src = (me + n - d) % n
-        remote(
-            norms.at[src], norms.at[src], norm_send.at[0], norm_recv.at[src],
-            {"img": partner},
-        ).wait_recv()
-        norm_row += norms[src][0:1, :]
-    norm = jnp.broadcast_to(norm_row, (LANES, poses)).T
     local_peak = None
     for t in range(trans):
-        value = scores[:, t * count : (t + 1) * count] - norm
-        scores[:, t * count : (t + 1) * count] = value
+        value = scores[:, t * count : (t + 1) * count]
         top = jnp.max(value, axis=0, keepdims=True)
         local_peak = top if local_peak is None else jnp.maximum(local_peak, top)
     local_sum = jnp.zeros((1, count), F32)
@@ -269,29 +306,16 @@
         scores[:, t * count : (t + 1) * count] = value
         local_sum += jnp.sum(value, axis=0, keepdims=True)
     row = lax.broadcasted_iota(jnp.int32, (8, count), 0)
-    stats[mine] = jnp.where(row == 0, local_peak, local_sum)
+    stats[mine, 0:8, :] = jnp.where(row == 0, local_peak, local_sum)
     for d in range(1, pn):
         send(
             stats.at[mine], stats.at[mine], stat_send.at[d - 1], stat_recv.at[mine],
             {"pose": (mine + d) % pn},
         )
 
-    for d in range(1, n):
-        src = (me + n - d) % n
-        remote(
-            seg,
-            seg_all.at[pl.ds(pl.multiple_of(src * share, 8), share)],
-            seg_send.at[0],
-            seg_recv.at[src],
-            {"img": partner},
-        ).wait_recv()
-    seg_t[...] = seg_all[...].T
-    message[...] = jnp.zeros_like(message)
-    for p in range(pn):
-        low = ((me * pn + p) * stencils).astype(F32)
-        named = seg_all[...]
-        inside = jnp.where((named >= low) & (named < low + stencils), 1.0, 0.0)
-        message[p, stencils : stencils + 1, 0:LANES] = jnp.sum(inside, axis=0, keepdims=True)
+    for copy in sends:
+        copy.wait_send()
+    sends.clear()
 
     for d in range(1, pn):
         src = (mine + pn - d) % pn
@@ -311,22 +335,20 @@
         at = slice(t * count, (t + 1) * count)
         post[:, at] = (scores[:, at] * factor).astype(BF16)
 
-    segments = part.shape[0]
     part[...] = jnp.zeros_like(part)
-    batch = 4 if nblk % 4 == 0 and segments <= 256 else 1
+    batch = 4 if nblk % 4 == 0 and kept == nblk else 1
 
     @pl.loop(0, nblk // batch)
     def _(q):
-        names = lax.broadcasted_iota(jnp.int32, (segments, poses), 0).astype(F32)
-        rows, picks = [], []
+        rows, chosen = [], []
         for u in range(batch):
             b = q * batch + u
             at = pl.multiple_of(b * block2, block2)
             sums = jnp.dot(post[...], weighted[:, pl.ds(at, block2)], preferred_element_type=F32)
             rows.append(sums.astype(BF16))
-            picks.append(jnp.where(names == seg_t[pl.ds(b, 1), :], 1.0, 0.0).astype(BF16))
+            chosen.append(picks[b] if kept == nblk else choose(b))
         part[...] += jnp.dot(
-            jnp.concatenate(picks, axis=1),
+            jnp.concatenate(chosen, axis=1),
             jnp.concatenate(rows, axis=0),
             preferred_element_type=F32,
         )
@@ -351,7 +373,7 @@
         ).wait_recv()
         summed += rows_in[src].astype(F32)
     for p in range(pn):
-        message[p, 0:stencils, :] = summed[p * stencils : (p + 1) * stencils, :]
+        message[p] = summed[p * stencils : (p + 1) * stencils, :]
     for d in range(1, pn):
         target = (mine + d) % pn
         send(
@@ -362,7 +384,14 @@
             {"pose": target},
         )
     brick = message[mine]
+    received = jnp.zeros((1, count), F32)
+    for p in range(pn):
+        received += stats[p, pl.ds(8 + mine, 1), :]
+    received = jnp.sum(received, axis=1, keepdims=True)
+    scale = lax.rsqrt(1.0 + jnp.broadcast_to(received, (1, volume.shape[1])))
     fetch.wait()
+    for copy in sends:
+        copy.wait_send()
     for d in range(1, pn):
         src = (mine + pn - d) % pn
         remote(
@@ -370,20 +399,12 @@
             {"pose": (mine + 1) % pn},
         ).wait_recv()
         brick += bricks_in[src]
-    gathered = brick[0:stencils, :].astype(BF16).astype(F32)
-    received = jnp.sum(brick[stencils : 2 * stencils, :])
-    row = lax.broadcasted_iota(jnp.int32, gathered.shape, 0)
-    out = jnp.zeros((stencils, volume.shape[1]), F32)
-    for s in range(stencils):
-        out += jnp.dot(
-            jnp.where(row == s, gathered, 0.0).astype(BF16),
-            matrices[s],
-            preferred_element_type=F32,
-        )
-    scale = lax.rsqrt(jnp.full((1, volume.shape[1]), 1.0, F32) + received)
+    row = lax.broadcasted_iota(jnp.int32, brick.shape, 0)
+    spread = jnp.concatenate(
+        [jnp.where(row == s, brick, 0.0).astype(BF16) for s in range(stencils)], axis=1
+    )
+    out = jnp.dot(spread, matrices[...], preferred_element_type=F32)
     volume[...] = jnp.sum(out, axis=0, keepdims=True) * scale
-    for copy in sends:
-        copy.wait_send()
 
 
 def body(images, shift_phase, noise_weight, refs, routing, stencil, interp):
@@ -396,34 +417,36 @@
     segments = n * pn * stencils
     nblk = pixels // LANES
     share = poses // n
-    seg = (routing[:, 0] * stencils + stencil).astype(F32).reshape(share, nblk)
-    seg = jnp.pad(seg, ((0, 0), (0, LANES - nblk)), constant_values=-1.0)
+    matrices = interp.reshape(stencils * 2 * LANES, interp.shape[3])
+    kept = nblk if segments <= 256 else 1
     vmem = pl.BlockSpec(memory_space=pltpu.VMEM)
     dma = pltpu.SemaphoreType.DMA
     flops = 4 * trans * count * width * poses
     volume, evidence = pl.pallas_call(
-        functools.partial(kernel, n, pn),
+        functools.partial(kernel, n, pn, stencils),
         out_shape=(
             jax.ShapeDtypeStruct((1, interp.shape[3]), F32),
             jax.ShapeDtypeStruct((1, count), F32),
         ),
-        in_specs=[vmem] * 5 + [pl.BlockSpec(memory_space=pl.ANY)],
+        in_specs=[vmem] * 6 + [pl.BlockSpec(memory_space=pl.ANY)],
         out_specs=(vmem, vmem),
         scratch_shapes=[
             pltpu.VMEM((n, 2, poses, depth // 2), BF16),
             pltpu.VMEM((trans * count, width), BF16),
             pltpu.VMEM((poses, trans * count), F32),
             pltpu.VMEM((poses, trans * count), BF16),
+            pltpu.VMEM((share, LANES), F32),
             pltpu.VMEM((poses, LANES), F32),
             pltpu.VMEM((LANES, poses), F32),
+            pltpu.VMEM((kept, segments, poses), BF16),
             pltpu.VMEM((n, 8, poses), F32),
-            pltpu.VMEM((pn, 8, count), F32),
+            pltpu.VMEM((pn, 8 + (pn + 7) // 8 * 8, count), F32),
             pltpu.VMEM((segments, 2 * LANES), F32),
             pltpu.VMEM((segments, 2 * LANES), BF16),
             pltpu.VMEM((n, pn * stencils, 2 * LANES), BF16),
-            pltpu.VMEM((pn, 2 * stencils, 2 * LANES), F32),
-            pltpu.VMEM((pn, 2 * stencils, 2 * LANES), F32),
-            pltpu.VMEM(interp.shape[1:], BF16),
+            pltpu.VMEM((pn, stencils, 2 * LANES), F32),
+            pltpu.VMEM((pn, stencils, 2 * LANES), F32),
+            pltpu.VMEM((stencils * 2 * LANES, interp.shape[3]), BF16),
             dma((n // 2, 2)),
             dma((n // 2, 2)),
             dma((2,)),
@@ -441,12 +464,12 @@
             dma,
         ],
         compiler_params=pltpu.CompilerParams(
-            collective_id=0, has_side_effects=True, vmem_limit_bytes=56 * 1024 * 1024
+            collective_id=0, has_side_effects=True, vmem_limit_bytes=46 * 1024 * 1024
         ),
         cost_estimate=pl.CostEstimate(
             flops=flops, bytes_accessed=8 * 1024 * 1024, transcendentals=trans * count * poses
         ),
-    )(images, shift_phase, noise_weight.reshape(1, width), refs, seg, interp[0])
+    )(images, shift_phase, noise_weight.reshape(1, width), refs, routing.reshape(share, nblk), stencil.reshape(share, nblk), matrices)
     return (volume, evidence.reshape(count))
 
 

time: 69.5 us -> 75.5 us (1.086)
  local copies, waits for them, and re-layouts: 3.09 us -> 7.91 us
  Pallas kernels: 64.1 us -> 65.8 us
    unnamed x2 -> x12, local copies, waits for them, and re-layouts: 2.41 us -> 7.07 us
    pallas_call x1, Pallas kernels: 64.1 us -> 65.8 us  [body(): pl.pallas_call(functools.partial(kernel, n, pn, stencils), out_shape=(jax...]
    reshape x1 -> x2, local copies, waits for them, and re-layouts: 0.07 us -> 0.84 us  [the longest x1 0.77 us: body(): stencil.reshape(share, nblk)]
where the time goes in v3:
time: 75.5 us; the launch traced here: 75.1 us
  Pallas kernels  65.8 us (87%)
  local copies, waits for them, and re-layouts  7.91 us (10%)
    pallas_call x1, Pallas kernels, body(): pl.pallas_call(functools.partial(kernel, n, pn, stencils), out_shape=(jax...  65.8 us
    unnamed x12, local copies, waits for them, and re-layouts  7.07 us

profile of v3, /device:TPU:0, one launch (start us, length us, event | category | flops | bytes accessed | tf_op | source)
XLA Modules:
  0.0 75.1 jit_solution(10524256619624078685)
XLA Ops:
  0.6 0.7 reduce
  1.3 0.1 reshape.20.routing
  1.4 0.8 %reshape.21.stencil = s32[48,32]{1,0:T(8,128)S(1)} reshape(s32[1536]{0:T(1024)} %param.12) | data formatting | bytes 12288 | tf_op jit(solution)/shard_map/reshape | solution.py:472
  2.2 0.0 copy-start
  2.2 1.6 %copy-done = bf16[128,8192]{1,0:T(8,128)(2,1)S(1)} copy-done((bf16[128,8192]{1,0:T(8,128)(2,1)S(1)}, bf16[128,8192]{1,0:T(8,128)(2,1)}, u32[]{:S(2)}) %copy-start) | copy-done | bytes 2097176
  3.8 0.0 copy-start.1
  3.8 1.6 %copy-done.1 = bf16[1,8,256,512]{3,2,1,0:T(8,128)(2,1)S(1)} copy-done((bf16[1,8,256,512]{3,2,1,0:T(8,128)(2,1)S(1)}, bf16[1,8,256,512]{3,2,1,0:T(8,128)(2,1)}, u32[]{:S(2)}) %copy-start.1) | copy-done | bytes 2097176
  5.4 0.0 copy-start.2
  5.4 1.1 %copy-done.2 = bf16[384,1024]{1,0:T(8,128)(2,1)S(1)} copy-done((bf16[384,1024]{1,0:T(8,128)(2,1)S(1)}, bf16[384,1024]{1,0:T(8,128)(2,1)}, u32[]{:S(2)}) %copy-start.2) | copy-done | bytes 786456
  6.5 0.0 copy-start.3
  6.5 0.9 %copy-done.3 = f32[8,4096]{1,0:T(8,128)S(1)} copy-done((f32[8,4096]{1,0:T(8,128)S(1)}, f32[8,4096]{1,0:T(8,128)}, u32[]{:S(2)}) %copy-start.3) | copy-done | bytes 131096
  7.4 0.0 copy-start.4
  7.4 0.8 %copy-done.4 = f32[8192]{0:T(1024)S(1)} copy-done((f32[8192]{0:T(1024)S(1)}, f32[8192]{0:T(1024)}, u32[]{:S(2)}) %copy-start.4) | copy-done | bytes 32792
  8.2 65.8 %shard_map.86 = (f32[1,512]{1,0:T(1,128)S(1)}, f32[1,128]{1,0:T(1,128)S(1)}) custom-call(bf16[128,8192]{1,0:T(8,128)(2,1)S(1)} %copy-done, f32[8,4096]{1,0:T(8,128)S(1)} %copy-done.3, f32[1,8192]{1,0:T(1,128)S(1)} %bitcast.4, bf16[384,1024]{1,0:T(8,128)(2,1)S(1)} %copy-done.2, s32[48,32]{1,0:T(8,128)S(1)} %reshape.20.routing, s32[48,32]{1,0:T(8,128)S(1)} %reshape.21.stencil, ...), custom_call_target="tpu_custom_call" | custom-call | flops 12884901888 | bytes 8388608 | tf_op jit(solution)/shard_map/pallas_call | solution.py:425
  74.0 0.6 copy.11
  74.6 0.5 copy.12
Async XLA Ops:
  2.2 1.6 %copy-start = (bf16[128,8192]{1,0:T(8,128)(2,1)S(1)}, bf16[128,8192]{1,0:T(8,128)(2,1)}, u32[]{:S(2)}) copy-start(bf16[128,8192]{1,0:T(8,128)(2,1)} %images.1) | copy-start | bytes 6291460
  3.8 1.6 %copy-start.1 = (bf16[1,8,256,512]{3,2,1,0:T(8,128)(2,1)S(1)}, bf16[1,8,256,512]{3,2,1,0:T(8,128)(2,1)}, u32[]{:S(2)}) copy-start(bf16[1,8,256,512]{3,2,1,0:T(8,128)(2,1)} %param.13) | copy-start | bytes 6291460
  5.4 1.1 %copy-start.2 = (bf16[384,1024]{1,0:T(8,128)(2,1)S(1)}, bf16[384,1024]{1,0:T(8,128)(2,1)}, u32[]{:S(2)}) copy-start(bf16[384,1024]{1,0:T(8,128)(2,1)} %refs.1) | copy-start | bytes 2359300
  6.5 0.9 %copy-start.3 = (f32[8,4096]{1,0:T(8,128)S(1)}, f32[8,4096]{1,0:T(8,128)}, u32[]{:S(2)}) copy-start(f32[8,4096]{1,0:T(8,128)} %phase.1) | copy-start | bytes 393220
  7.4 0.8 %copy-start.4 = (f32[8192]{0:T(1024)S(1)}, f32[8192]{0:T(1024)}, u32[]{:S(2)}) copy-start(f32[8192]{0:T(1024)} %param.9) | copy-start | bytes 98308

commit v4 on v3

--- a/solution.py
+++ b/solution.py
@@ -257,23 +257,23 @@
             multiply(cols[partner, h], partner, h)
         multiply(cols[near_x, 0], near_x, 0)
         multiply(cols[near_y, 0], near_y, 0)
+        arrived(near_y, 1)
+        send(
+            cols.at[near_y, 1], cols.at[near_y, 1], diag_send.at[1],
+            gather_recv.at[near_y, 1], {"img": near_x},
+        )
+        hand_over(near_y, 1, 1)
+        arrived(near_x, 1)
+        hand_over(near_x, 1, 0)
         for src in (near_x, near_y):
             arrived(other_core(src), 0)
             multiply(cols[other_core(src), 0], other_core(src), 0)
-        prepare()
-        arrived(near_y, 1)
-        send(
-            cols.at[near_y, 1], cols.at[near_y, 1], diag_send.at[1],
-            gather_recv.at[near_y, 1], {"img": near_x},
-        )
-        hand_over(near_y, 1, 1)
-        arrived(near_x, 1)
-        hand_over(near_x, 1, 0)
         for src in (near_y, near_x):
             multiply(cols[src, 1], src, 1)
         for src in (near_y, near_x):
             arrived(other_core(src), 1)
             multiply(cols[other_core(src), 1], other_core(src), 1)
+        prepare()
         for h in range(2):
             arrived(diag, h)
             hand_over(diag, h, 2)
@@ -464,7 +464,7 @@
             dma,
         ],
         compiler_params=pltpu.CompilerParams(
-            collective_id=0, has_side_effects=True, vmem_limit_bytes=46 * 1024 * 1024
+            collective_id=0, has_side_effects=True, vmem_limit_bytes=56 * 1024 * 1024
         ),
         cost_estimate=pl.CostEstimate(
             flops=flops, bytes_accessed=8 * 1024 * 1024, transcendentals=trans * count * poses

time: 75.5 us -> 70.1 us (0.928)
  local copies, waits for them, and re-layouts: 7.91 us -> 4.39 us
  Pallas kernels: 65.8 us -> 64 us
    unnamed x12 -> x2, local copies, waits for them, and re-layouts: 7.07 us -> 2.35 us
    pallas_call x1, Pallas kernels: 65.8 us -> 64 us  [body(): pl.pallas_call(functools.partial(kernel, n, pn, stencils), out_shape=(jax...]
where the time goes in v4:
time: 70.1 us; the launch traced here: 69.8 us
  Pallas kernels  64 us (91%)
  local copies, waits for them, and re-layouts  4.39 us (6%)
  other arithmetic  0.71 us (1%)
    pallas_call x1, Pallas kernels, body(): pl.pallas_call(functools.partial(kernel, n, pn, stencils), out_shape=(jax...  64 us
    unnamed x2, local copies, waits for them, and re-layouts  2.35 us

profile of v4, /device:TPU:0, one launch (start us, length us, event | category | flops | bytes accessed | tf_op | source)
XLA Modules:
  0.0 69.8 jit_solution(8525817530349807269)
XLA Ops:
  0.6 0.7 %reduce = s32[1536]{0:T(1024)S(1)} reduce(s32[1536,1]{0,1:T(1,128)} %param.11, s32[]{:T(128)} %constant.1), dimensions={1}, to_apply=%param.11.reduce_sub_computation | reduce | bytes 12292 | tf_op args[4]
  1.3 0.7 reshape.20.routing
  2.0 1.4 %reshape.21.stencil = s32[48,32]{1,0:T(8,128)} reshape(s32[1536]{0:T(1024)} %param.12) | data formatting | bytes 12288 | tf_op jit(solution)/shard_map/reshape | solution.py:472
  3.4 64.0 %shard_map.86 = (f32[1,512]{1,0:T(1,128)}, f32[1,128]{1,0:T(1,128)}) custom-call(bf16[128,8192]{1,0:T(8,128)(2,1)} %images.1, f32[8,4096]{1,0:T(8,128)} %phase.1, f32[1,8192]{1,0:T(1,128)} %bitcast.4, bf16[384,1024]{1,0:T(8,128)(2,1)} %refs.1, s32[48,32]{1,0:T(8,128)} %reshape.20.routing, s32[48,32]{1,0:T(8,128)} %reshape.21.stencil, bf16[2048,512]{1,0:T(8,128)(2,1)} %bitcast.3), custom_call_target="tpu_custom_call" | custom-call | flops 12884901888 | bytes 8388608 | tf_op jit(solution)/shard_map/pallas_call | solution.py:425
  67.4 1.2 %copy.11 = f32[1,512]{1,0:T(1,128)} copy(f32[1,512]{1,0:T(1,128)} %get-tuple-element.8) | data formatting | bytes 4096
  68.7 1.1 %copy.12 = f32[128]{0:T(128)} copy(f32[128]{0:T(128)} %bitcast.5) | data formatting | bytes 1024
